TPU v7x, 32 devices: a whole 2x2x4 slice. The times are simulated.
32 devices in a mesh: row: 8 (over z, x), col: 4 (over y, core).
Axes of the slice: x: 2, y: 2, z: 4, core: 2. Of those that a mesh axis runs over, the one named last changes fastest.
Arguments:
- log_rate: float32 [131072], P(('row', 'col')), may hold values from -0.5 to 1
- state: float32 [131072], P(('row', 'col')), may hold values from 0.2 to 1
- excess: float32 [131072], P(('row', 'col')), may hold values from -0.3 to 0.3
- normal_stress: float32 [131072], P(('row', 'col')), may hold values from 2 to 4
- rate_param: float32 [131072], P(('row', 'col')), may hold values from 0.5 to 1
- state_param: float32 [131072], P(('row', 'col')), may hold values from 0.5 to 1.5
- slip_length: float32 [131072], P(('row', 'col')), may hold values from 1 to 4
- self_stiffness: float32 [131072], P(('row', 'col')), may hold values from 0.2 to 1
- damping: float32 [131072], P(('row', 'col')), may hold values from 1 to 2
- blocks: bfloat16 [8, 4, 512, 4096], P('row', 'col'), may hold values from -0.1796875 to 0.1796875
- pattern: int32 [8, 4, 512, 2], P('row', 'col'), may hold values from 0 to 511
- counts: int32 [8, 4], P('row', 'col'), may hold values from 1 to 512, as said below
Outputs:
- final_log_rate: float32 [131072], P(('row', 'col'))
- final_state: float32 [131072], P(('row', 'col'))
- final_stress: float32 [131072], P(('row', 'col'))
Inputs may be any that keep to these rules, and one draw needn't show every extreme that they name: `counts`: every device holds at least one live tile; some device of the first index of row holds 512.
All inputs are finite; a program needn't handle non-finite values.
Results may differ from a plain program's by a relative error of at most 0.0014.
Values may be sent and summed in bfloat16 or wider, within the bound.
A program may use at most 64 MiB of HBM per device.

v0:
```python
import functools

import jax
import jax.numpy as jnp
from jax import lax
from jax.experimental import pallas as pl
from jax.experimental.pallas import tpu as pltpu
from jax.sharding import PartitionSpec as P

STEPS = 2
NEWTON = 4
EDGE = 64
LANES = 128
SPAN = 512
MESH = pl.DeviceIdType.MESH

time_step = 0.25


def inverse_sinh(value):
    return jnp.log(value + jnp.sqrt(1.0 + value * value))


def friction_solve(rate_log, stress, state, normal_stress, rate_param, damping):
    for turn_index in range(NEWTON):
        speed = jnp.exp(rate_log)
        ratio = 0.5 * jnp.exp(rate_log + state / rate_param)
        misfit = stress - damping * speed - normal_stress * rate_param * inverse_sinh(ratio)
        slope = -damping * speed - normal_stress * rate_param * ratio / jnp.sqrt(
            1.0 + ratio * ratio
        )
        rate_log = rate_log - misfit / slope
    return rate_log


def dot(left, right):
    return jnp.dot(left, right, preferred_element_type=jnp.float32)


def twice(pieces):
    count, half, lanes = pieces.shape
    flat = pieces.astype(jnp.float32).reshape(count * half, lanes)
    other = pltpu.roll(flat, EDGE, 1)
    low = lax.broadcasted_iota(jnp.int32, flat.shape, 1) < EDGE
    even = jnp.where(low, flat, other).reshape(count, half, lanes)
    odd = jnp.where(low, other, flat).reshape(count, half, lanes)
    both = jnp.concatenate([even, odd], axis=1)
    return both.reshape(count * 2 * half, lanes).astype(jnp.bfloat16)


def scatter(onehot, values, count, half):
    high = values.astype(jnp.bfloat16)
    rest = values - high.astype(jnp.float32)
    middle = rest.astype(jnp.bfloat16)
    low = (rest - middle.astype(jnp.float32)).astype(jnp.bfloat16)
    sums = dot(onehot, jnp.concatenate([high, middle, low], axis=1))
    sums = sums[:, :LANES] + sums[:, LANES : 2 * LANES] + sums[:, 2 * LANES :]
    sums = sums.reshape(count, 2, half, LANES)
    even, odd = sums[:, 0], sums[:, 1]
    return jnp.where(lax.broadcasted_iota(jnp.int32, even.shape, 2) < EDGE, even, odd)


def body(
    rows,
    cols,
    counts_ref,
    pattern_hbm,
    log_rate_hbm,
    state_hbm,
    excess_hbm,
    normal_hbm,
    rate_param_hbm,
    state_param_hbm,
    slip_hbm,
    stiff_hbm,
    damping_hbm,
    blocks_ref,
    final_ref,
    inputs,
    pattern_ref,
    tiles,
    row_pick,
    col_pick,
    row_place,
    col_place,
    spread,
    gather_sum,
    row_tab,
    col_tab,
    row_send,
    col_send,
    row_land,
    col_land,
    tile_sem,
    input_sem,
    sems_row_tab,
    sems_col_tab,
    sems_row_part,
    sems_col_part,
):
    my_row = lax.axis_index("row")
    my_col = lax.axis_index("col")
    half = log_rate_hbm.shape[0]
    per_seg = 2 * half
    slots, width = tiles.shape
    groups = tile_sem.shape[0]
    depth = slots // groups

    barrier = pltpu.get_barrier_semaphore()
    for k in range(1, cols):
        pl.semaphore_signal(
            barrier, inc=1, device_id={"col": lax.rem(my_col + k, cols)}, device_id_type=MESH
        )
    for k in range(1, rows):
        pl.semaphore_signal(
            barrier, inc=1, device_id={"row": lax.rem(my_row + k, rows)}, device_id_type=MESH
        )

    def tile_copy(group):
        part = pl.ds(group * depth, depth)
        return pltpu.make_async_copy(blocks_ref.at[part], tiles.at[part], tile_sem.at[group])

    vectors = (
        log_rate_hbm,
        state_hbm,
        excess_hbm,
        normal_hbm,
        rate_param_hbm,
        state_param_hbm,
        slip_hbm,
        stiff_hbm,
        damping_hbm,
    )
    input_copies = [
        pltpu.make_async_copy(vector, inputs.at[index], input_sem.at[index])
        for index, vector in enumerate(vectors)
    ]
    input_copies.append(
        pltpu.make_async_copy(pattern_hbm, pattern_ref, input_sem.at[len(vectors)])
    )
    for copy in input_copies:
        copy.start()
    for group in range(groups):
        tile_copy(group).start()
    for copy in input_copies:
        copy.wait()
    rate_in, state_in, excess_ref, normal_in, rate_param_in = (inputs.at[n] for n in range(5))
    state_param_ref, slip_ref, stiff_ref, damping_in = (inputs.at[n] for n in range(5, 9))
    rate_ref, state_ref, stress_ref, normal_ref, rate_param_ref, damping_ref = (
        final_ref.at[n] for n in range(6)
    )
    normal_ref[...] = normal_in[...]
    rate_param_ref[...] = rate_param_in[...]
    damping_ref[...] = damping_in[...]
    rate_log = rate_in[...]
    state = state_in[...]
    rate_param = rate_param_ref[...]
    balance = normal_ref[...] * rate_param * inverse_sinh(
        0.5 * jnp.exp(rate_log + state / rate_param)
    ) + damping_ref[...] * jnp.exp(rate_log)
    rate_ref[...] = rate_log
    state_ref[...] = state
    stress_ref[...] = balance * (1.0 + excess_ref[...])

    row_slot = pattern_ref[0:1, :]
    col_slot = pattern_ref[1:2, :]
    active = lax.broadcasted_iota(jnp.int32, (1, slots), 1) < counts_ref[0, 0]
    diagonal = (col_slot // per_seg == my_row) & (
        row_slot == my_col * per_seg + col_slot % per_seg
    )

    def position(block):
        inner = block % per_seg
        return (block // per_seg) * per_seg + (inner % 2) * half + inner // 2

    def fill(place, pick, block, keep):
        total = place.shape[0]
        hit = position(block) == lax.broadcasted_iota(jnp.int32, (total, slots), 0)
        ones = jnp.where(hit, 1.0, 0.0)
        pick[...] = ones.T.astype(jnp.bfloat16)
        place[...] = jnp.where(keep, ones, 0.0).astype(jnp.bfloat16)

    fill(row_place, row_pick, row_slot, active)
    fill(col_place, col_pick, col_slot, active & jnp.logical_not(diagonal))
    spread[...] = jnp.where(
        lax.broadcasted_iota(jnp.int32, spread.shape, 0)
        == lax.broadcasted_iota(jnp.int32, spread.shape, 1) // EDGE,
        1.0,
        0.0,
    ).astype(jnp.bfloat16)
    gather_sum[...] = jnp.where(
        lax.broadcasted_iota(jnp.int32, gather_sum.shape, 0) // EDGE
        == lax.broadcasted_iota(jnp.int32, gather_sum.shape, 1) % EDGE,
        1.0,
        0.0,
    ).astype(jnp.bfloat16)

    def tab_copy(step, axis, k, sender):
        tab, sems, me, count = (
            (row_tab, sems_row_tab, my_col, cols)
            if axis == "col"
            else (col_tab, sems_col_tab, my_row, rows)
        )
        slot = me if sender else lax.rem(me - k + count, count)
        return pltpu.make_async_remote_copy(
            src_ref=tab.at[step, slot],
            dst_ref=tab.at[step, slot],
            send_sem=sems.at[0, step, k],
            recv_sem=sems.at[1, step, k],
            device_id={axis: lax.rem(me + k, count)},
            device_id_type=MESH,
        )

    def part_copy(step, axis, k):
        send, land, sems, me, count = (
            (row_send, row_land, sems_row_part, my_col, cols)
            if axis == "col"
            else (col_send, col_land, sems_col_part, my_row, rows)
        )
        target = lax.rem(me + k, count)
        return pltpu.make_async_remote_copy(
            src_ref=send.at[step, target],
            dst_ref=land.at[step, k - 1],
            send_sem=sems.at[0, step, k],
            recv_sem=sems.at[1, step, k],
            device_id={axis: target},
            device_id_type=MESH,
        )

    pl.semaphore_wait(barrier, rows + cols - 2)

    def one_step(step, carry):
        rate_log = rate_ref[...]
        speed = jnp.exp(rate_log)
        pushed = (speed - 1.0).astype(jnp.bfloat16)
        row_tab[step, my_col] = pushed
        col_tab[step, my_row] = pushed
        for k in range(1, rows):
            tab_copy(step, "row", k, True).start()
        for k in range(1, cols):
            tab_copy(step, "col", k, True).start()

        @pl.when(step == 0)
        def _():
            for group in range(groups):
                tile_copy(group).wait()

        for k in range(1, cols):
            tab_copy(step, "col", k, False).wait_recv()
        row_values = dot(row_pick[...], twice(row_tab[step])).astype(jnp.bfloat16)

        def mirror_turn(turn, total):
            part = pl.ds(pl.multiple_of(turn * SPAN, SPAN), SPAN)
            product = tiles[:, part].astype(jnp.float32) * dot(row_values, spread[:, part])
            for c in range(SPAN // LANES):
                total = total + product[:, c * LANES : (c + 1) * LANES]
            return total

        zero = jnp.zeros((slots, LANES), jnp.float32)
        mirror = lax.fori_loop(0, width // SPAN, mirror_turn, zero)
        mirror = mirror + pltpu.roll(mirror, EDGE, 1)
        col_send[step] = scatter(col_place[...], mirror, rows, half)
        for k in range(1, rows):
            part_copy(step, "row", k).start()

        for k in range(1, rows):
            tab_copy(step, "row", k, False).wait_recv()
        col_values = dot(col_pick[...], twice(col_tab[step]))

        def direct_turn(turn, total):
            part = pl.ds(pl.multiple_of(turn * SPAN, SPAN), SPAN)
            product = tiles[:, part].astype(jnp.float32) * jnp.concatenate(
                [col_values] * (SPAN // LANES), axis=1
            )
            high = product.astype(jnp.bfloat16)
            low = (product - high.astype(jnp.float32)).astype(jnp.bfloat16)
            adder = gather_sum[part, :]
            return total + (dot(high, adder) + dot(low, adder))

        direct = lax.fori_loop(0, width // SPAN, direct_turn, zero)
        row_send[step] = scatter(row_place[...], direct, cols, half)
        for k in range(1, cols):
            part_copy(step, "col", k).start()

        state = state_ref[...]
        state_param = state_param_ref[...]
        new_state = state + time_step * (state_param / slip_ref[...]) * (
            jnp.exp(-state / state_param) - speed
        )
        stress_rate = col_send[step, my_row] + row_send[step, my_col]
        for k in range(1, rows):
            part_copy(step, "row", k).wait_recv()
            stress_rate = stress_rate + col_land[step, k - 1]
        for k in range(1, cols):
            part_copy(step, "col", k).wait_recv()
            stress_rate = stress_rate + row_land[step, k - 1]
        stress = stress_ref[...] + time_step * (stress_rate - stiff_ref[...] * (speed - 1.0))
        state_ref[...] = new_state
        stress_ref[...] = stress

        @pl.when(step < STEPS - 1)
        def _():
            rate_ref[...] = friction_solve(
                rate_log, stress, new_state, normal_ref[...], rate_param_ref[...], damping_ref[...]
            )

        for k in range(1, rows):
            tab_copy(step, "row", k, True).wait_send()
            part_copy(step, "row", k).wait_send()
        for k in range(1, cols):
            tab_copy(step, "col", k, True).wait_send()
            part_copy(step, "col", k).wait_send()
        return carry

    lax.fori_loop(0, STEPS, one_step, 0)


def finish(final_ref, rate_ref, state_ref, stress_ref):
    rate_log, state, stress, normal_stress, rate_param, damping = (final_ref[n] for n in range(6))
    state_ref[...] = state
    stress_ref[...] = stress
    rate_ref[...] = friction_solve(rate_log, stress, state, normal_stress, rate_param, damping)


def on_device(*arguments):
    vectors, (blocks, pattern, counts) = arguments[:9], arguments[9:]
    rows = lax.axis_size("row")
    cols = lax.axis_size("col")
    patches = vectors[0].shape[0]
    shape = (patches // LANES, LANES)
    half = shape[0]
    slots, width = blocks.shape[2], blocks.shape[3]
    blocks_row = cols * 2 * half
    blocks_col = rows * 2 * half
    vmem = pl.BlockSpec(memory_space=pltpu.VMEM)
    bf16, f32 = jnp.bfloat16, jnp.float32
    hbm = pl.BlockSpec(memory_space=pltpu.HBM)
    final = pl.pallas_call(
        functools.partial(body, rows, cols),
        out_shape=jax.ShapeDtypeStruct((6,) + shape, f32),
        in_specs=[pl.BlockSpec(memory_space=pltpu.SMEM)] + [hbm] * 11,
        out_specs=vmem,
        scratch_shapes=[
            pltpu.VMEM((9,) + shape, f32),
            pltpu.VMEM((2, slots), jnp.int32),
            pltpu.VMEM((slots, width), bf16),
            pltpu.VMEM((slots, blocks_row), bf16),
            pltpu.VMEM((slots, blocks_col), bf16),
            pltpu.VMEM((blocks_row, slots), bf16),
            pltpu.VMEM((blocks_col, slots), bf16),
            pltpu.VMEM((LANES, width), bf16),
            pltpu.VMEM((width, LANES), bf16),
            pltpu.VMEM((STEPS, cols) + shape, bf16),
            pltpu.VMEM((STEPS, rows) + shape, bf16),
            pltpu.VMEM((STEPS, cols) + shape, f32),
            pltpu.VMEM((STEPS, rows) + shape, f32),
            pltpu.VMEM((STEPS, cols - 1) + shape, f32),
            pltpu.VMEM((STEPS, rows - 1) + shape, f32),
            pltpu.SemaphoreType.DMA((4,)),
            pltpu.SemaphoreType.DMA((10,)),
            pltpu.SemaphoreType.DMA((2, STEPS, cols)),
            pltpu.SemaphoreType.DMA((2, STEPS, rows)),
            pltpu.SemaphoreType.DMA((2, STEPS, cols)),
            pltpu.SemaphoreType.DMA((2, STEPS, rows)),
        ],
        compiler_params=pltpu.CompilerParams(
            collective_id=0, has_side_effects=True, vmem_limit_bytes=60 * 1024 * 1024
        ),
    )(
        counts,
        pattern.reshape(slots, 2).T,
        *[vector.reshape(shape) for vector in vectors],
        blocks.reshape(slots, width),
    )
    outputs = pl.pallas_call(
        finish,
        out_shape=[jax.ShapeDtypeStruct(shape, f32)] * 3,
        in_specs=[vmem],
        out_specs=[vmem] * 3,
    )(final)
    return tuple(output.reshape(patches) for output in outputs)


def solution(mesh):
    patches = P(("row", "col"))
    in_specs = (patches,) * 9 + (
        P("row", "col", None, None),
        P("row", "col", None, None),
        P("row", "col"),
    )
    return jax.shard_map(
        on_device, mesh=mesh, in_specs=in_specs, out_specs=(patches,) * 3, check_vma=False
    )
```

profile of v0, /device:TPU:0, one launch (start us, length us, event | category | flops | bytes accessed | tf_op | source)
XLA Modules:
  0.0 37.6 jit_solution(6961530982139496660)
XLA Ops:
  1.3 34.7 %shard_map.139.final_ref = f32[6,32,128]{2,1,0:T(8,128)} custom-call(s32[1,1]{1,0:T(1,128)S(6)} %copy.15.counts_ref, s32[2,512]{1,0:T(2,128)} %bitcast.26, f32[32,128]{1,0:T(8,128)} %bitcast.17, f32[32,128]{1,0:T(8,128)} %bitcast.18, f32[32,128]{1,0:T(8,128)} %bitcast.19, f32[32,128]{1,0:T(8,128)} %bitcast.20, f32[32,128]{1,0:T(8,128)} %bitcast.21, ...), custom_call_target="tpu_custom_call" | custom-call | tf_op jit(solution)/shard_map/pallas_call | solution.py:338
  36.0 1.7 %shard_map.140 = (f32[32,128]{1,0:T(8,128)}, f32[32,128]{1,0:T(8,128)}, f32[32,128]{1,0:T(8,128)}) custom-call(f32[6,32,128]{2,1,0:T(8,128)} %shard_map.139.final_ref), custom_call_target="tpu_custom_call" | custom-call | tf_op jit(solution)/shard_map/pallas_call | solution.py:375
where the time goes:
time: 37.9 us; the launch traced here: 37.6 us
  Pallas kernels  36.4 us (96%)
  between operations  1.29 us (3%)
    pallas_call x1, Pallas kernels, on_device(): pl.pallas_call(functools.partial(body, rows, cols), out_shape=jax.ShapeDt...  34.7 us
    pallas_call x1, Pallas kernels, on_device(): pl.pallas_call(finish, out_shape=[jax.ShapeDtypeStruct(shape, f32)] * 3,...  1.65 us

commit v1 on v0

--- a/solution.py
+++ b/solution.py
@@ -12,6 +12,8 @@
 EDGE = 64
 LANES = 128
 SPAN = 512
+QUAD = 4
+GROUP = LANES // QUAD
 MESH = pl.DeviceIdType.MESH
 
 time_step = 0.25
@@ -48,13 +50,20 @@
     return both.reshape(count * 2 * half, lanes).astype(jnp.bfloat16)
 
 
-def scatter(onehot, values, count, half):
+def three_terms(values):
     high = values.astype(jnp.bfloat16)
     rest = values - high.astype(jnp.float32)
     middle = rest.astype(jnp.bfloat16)
     low = (rest - middle.astype(jnp.float32)).astype(jnp.bfloat16)
-    sums = dot(onehot, jnp.concatenate([high, middle, low], axis=1))
-    sums = sums[:, :LANES] + sums[:, LANES : 2 * LANES] + sums[:, 2 * LANES :]
+    return [high, middle, low]
+
+
+def scatter(onehot, values):
+    sums = dot(onehot, jnp.concatenate(three_terms(values), axis=1))
+    return sums[:, :LANES] + sums[:, LANES : 2 * LANES] + sums[:, 2 * LANES :]
+
+
+def paired(sums, count, half):
     sums = sums.reshape(count, 2, half, LANES)
     even, odd = sums[:, 0], sums[:, 1]
     return jnp.where(lax.broadcasted_iota(jnp.int32, even.shape, 2) < EDGE, even, odd)
@@ -80,11 +89,12 @@
     pattern_ref,
     tiles,
     row_pick,
-    col_pick,
-    row_place,
+    col_find,
     col_place,
     spread,
-    gather_sum,
+    weights,
+    picked,
+    turned,
     row_tab,
     col_tab,
     row_send,
@@ -173,28 +183,20 @@
         inner = block % per_seg
         return (block // per_seg) * per_seg + (inner % 2) * half + inner // 2
 
-    def fill(place, pick, block, keep):
-        total = place.shape[0]
+    def onehot(block, total):
         hit = position(block) == lax.broadcasted_iota(jnp.int32, (total, slots), 0)
-        ones = jnp.where(hit, 1.0, 0.0)
-        pick[...] = ones.T.astype(jnp.bfloat16)
-        place[...] = jnp.where(keep, ones, 0.0).astype(jnp.bfloat16)
-
-    fill(row_place, row_pick, row_slot, active)
-    fill(col_place, col_pick, col_slot, active & jnp.logical_not(diagonal))
+        return jnp.where(hit & active, 1.0, 0.0)
+
+    row_pick[...] = onehot(row_slot, row_pick.shape[1]).T.astype(jnp.bfloat16)
+    found = onehot(col_slot, col_place.shape[0])
+    col_find[...] = found.astype(jnp.bfloat16)
+    col_place[...] = jnp.where(diagonal, 0.0, found).astype(jnp.bfloat16)
     spread[...] = jnp.where(
         lax.broadcasted_iota(jnp.int32, spread.shape, 0)
         == lax.broadcasted_iota(jnp.int32, spread.shape, 1) // EDGE,
         1.0,
         0.0,
     ).astype(jnp.bfloat16)
-    gather_sum[...] = jnp.where(
-        lax.broadcasted_iota(jnp.int32, gather_sum.shape, 0) // EDGE
-        == lax.broadcasted_iota(jnp.int32, gather_sum.shape, 1) % EDGE,
-        1.0,
-        0.0,
-    ).astype(jnp.bfloat16)
-
     def tab_copy(step, axis, k, sender):
         tab, sems, me, count = (
             (row_tab, sems_row_tab, my_col, cols)
@@ -259,26 +261,69 @@
         zero = jnp.zeros((slots, LANES), jnp.float32)
         mirror = lax.fori_loop(0, width // SPAN, mirror_turn, zero)
         mirror = mirror + pltpu.roll(mirror, EDGE, 1)
-        col_send[step] = scatter(col_place[...], mirror, rows, half)
+        col_send[step] = paired(scatter(col_place[...], mirror), rows, half)
         for k in range(1, rows):
             part_copy(step, "row", k).start()
 
         for k in range(1, rows):
             tab_copy(step, "row", k, False).wait_recv()
-        col_values = dot(col_pick[...], twice(col_tab[step]))
-
-        def direct_turn(turn, total):
-            part = pl.ds(pl.multiple_of(turn * SPAN, SPAN), SPAN)
-            product = tiles[:, part].astype(jnp.float32) * jnp.concatenate(
-                [col_values] * (SPAN // LANES), axis=1
+        values = lax.dot_general(
+            twice(col_tab[step]),
+            col_find[...],
+            (((0,), (0,)), ((), ())),
+            preferred_element_type=jnp.float32,
+        )[:EDGE]
+        section = lax.broadcasted_iota(jnp.int32, (EDGE, LANES), 1) // GROUP
+        for base in range(slots // LANES):
+            part = values[:, base * LANES : (base + 1) * LANES]
+            shifted = [part] + [pltpu.roll(part, n * GROUP, 1) for n in range(1, QUAD)]
+            for inner in range(QUAD):
+                weights[base * QUAD + inner] = jnp.concatenate(
+                    [
+                        jnp.where(section == q, shifted[(q - inner) % QUAD], 0.0)
+                        for q in range(QUAD)
+                    ],
+                    axis=0,
+                ).astype(jnp.bfloat16)
+
+        own = lax.broadcasted_iota(jnp.int32, (1, GROUP, LANES), 1) == (
+            lax.broadcasted_iota(jnp.int32, (1, GROUP, LANES), 2) % GROUP
+        )
+        wide = QUAD * EDGE
+        fours = width // wide
+
+        def direct_turn(group, carry):
+            part = tiles[pl.ds(pl.multiple_of(group * GROUP, GROUP), GROUP), :]
+            stacked = jnp.concatenate(
+                [part[:, n * wide : (n + 1) * wide] for n in range(fours)], axis=0
             )
-            high = product.astype(jnp.bfloat16)
-            low = (product - high.astype(jnp.float32)).astype(jnp.bfloat16)
-            adder = gather_sum[part, :]
-            return total + (dot(high, adder) + dot(low, adder))
-
-        direct = lax.fori_loop(0, width // SPAN, direct_turn, zero)
-        row_send[step] = scatter(row_place[...], direct, cols, half)
+            product = dot(stacked, weights[group]).reshape(fours, GROUP, LANES)
+            picked[group] = jnp.sum(jnp.where(own, product, 0.0), axis=1)
+            return carry
+
+        lax.fori_loop(0, slots // GROUP, direct_turn, 0)
+        narrow = lax.broadcasted_iota(jnp.int32, (fours, LANES), 1) // GROUP
+        pieces = [[] for q in range(QUAD)]
+        for base in range(slots // LANES):
+            parts = [picked[base * QUAD + inner] for inner in range(QUAD)]
+            for q in range(QUAD):
+                joined = jnp.zeros((fours, LANES), jnp.float32)
+                for inner in range(QUAD):
+                    shift = (inner - q) % QUAD * GROUP
+                    moved = pltpu.roll(parts[inner], shift, 1) if shift else parts[inner]
+                    joined = jnp.where(narrow == inner, moved, joined)
+                pieces[q].append(joined)
+        direct = jnp.concatenate([jnp.concatenate(part, axis=1) for part in pieces], axis=0)
+        sums = dot(jnp.concatenate(three_terms(direct), axis=0), row_pick[...])
+        sums = sums[:EDGE] + sums[EDGE : 2 * EDGE] + sums[2 * EDGE :]
+        for q in range(QUAD):
+            for copied in range(LANES // EDGE):
+                for chunk in range(turned.shape[0]):
+                    turned[chunk, pl.ds(copied * EDGE + q, fours, QUAD), :] = sums[
+                        q * fours : (q + 1) * fours, chunk * LANES : (chunk + 1) * LANES
+                    ]
+        back = jnp.concatenate([turned[chunk].T for chunk in range(turned.shape[0])], axis=0)
+        row_send[step] = paired(back, cols, half)
         for k in range(1, cols):
             part_copy(step, "col", k).start()
 
@@ -345,11 +390,12 @@
             pltpu.VMEM((2, slots), jnp.int32),
             pltpu.VMEM((slots, width), bf16),
             pltpu.VMEM((slots, blocks_row), bf16),
-            pltpu.VMEM((slots, blocks_col), bf16),
-            pltpu.VMEM((blocks_row, slots), bf16),
+            pltpu.VMEM((blocks_col, slots), bf16),
             pltpu.VMEM((blocks_col, slots), bf16),
             pltpu.VMEM((LANES, width), bf16),
-            pltpu.VMEM((width, LANES), bf16),
+            pltpu.VMEM((slots // GROUP, QUAD * EDGE, LANES), bf16),
+            pltpu.VMEM((slots // GROUP, width // (QUAD * EDGE), LANES), f32),
+            pltpu.VMEM((blocks_row // LANES, LANES, LANES), f32),
             pltpu.VMEM((STEPS, cols) + shape, bf16),
             pltpu.VMEM((STEPS, rows) + shape, bf16),
             pltpu.VMEM((STEPS, cols) + shape, f32),

time: 37.9 us -> 37.8 us (level)
  no operation moved by 1% of the time
where the time goes in v1:
time: 37.8 us; the launch traced here: 37.5 us
  Pallas kernels  36.2 us (96%)
  between operations  1.29 us (3%)
    pallas_call x1, Pallas kernels, on_device(): pl.pallas_call(functools.partial(body, rows, cols), out_shape=jax.ShapeDt...  34.6 us
    pallas_call x1, Pallas kernels, on_device(): pl.pallas_call(finish, out_shape=[jax.ShapeDtypeStruct(shape, f32)] * 3,...  1.65 us

profile of v1, /device:TPU:0, one launch (start us, length us, event | category | flops | bytes accessed | tf_op | source)
XLA Modules:
  0.0 37.5 jit_solution(5144829703434644919)
XLA Ops:
  1.3 34.6 %shard_map.139.final_ref = f32[6,32,128]{2,1,0:T(8,128)} custom-call(s32[1,1]{1,0:T(1,128)S(6)} %copy.15.counts_ref, s32[2,512]{1,0:T(2,128)} %bitcast.26, f32[32,128]{1,0:T(8,128)} %bitcast.17, f32[32,128]{1,0:T(8,128)} %bitcast.18, f32[32,128]{1,0:T(8,128)} %bitcast.19, f32[32,128]{1,0:T(8,128)} %bitcast.20, f32[32,128]{1,0:T(8,128)} %bitcast.21, ...), custom_call_target="tpu_custom_call" | custom-call | tf_op jit(solution)/shard_map/pallas_call | solution.py:383
  35.9 1.7 %shard_map.140 = (f32[32,128]{1,0:T(8,128)}, f32[32,128]{1,0:T(8,128)}, f32[32,128]{1,0:T(8,128)}) custom-call(f32[6,32,128]{2,1,0:T(8,128)} %shard_map.139.final_ref), custom_call_target="tpu_custom_call" | custom-call | tf_op jit(solution)/shard_map/pallas_call | solution.py:421

commit v2 on v1

--- a/solution.py
+++ b/solution.py
@@ -11,7 +11,8 @@
 NEWTON = 4
 EDGE = 64
 LANES = 128
-SPAN = 512
+SPAN = 256
+STRIP = 128
 QUAD = 4
 GROUP = LANES // QUAD
 MESH = pl.DeviceIdType.MESH
@@ -92,6 +93,8 @@
     col_find,
     col_place,
     spread,
+    spread_in,
+    mirrored,
     weights,
     picked,
     turned,
@@ -159,18 +162,7 @@
     rate_ref, state_ref, stress_ref, normal_ref, rate_param_ref, damping_ref = (
         final_ref.at[n] for n in range(6)
     )
-    normal_ref[...] = normal_in[...]
-    rate_param_ref[...] = rate_param_in[...]
-    damping_ref[...] = damping_in[...]
-    rate_log = rate_in[...]
-    state = state_in[...]
-    rate_param = rate_param_ref[...]
-    balance = normal_ref[...] * rate_param * inverse_sinh(
-        0.5 * jnp.exp(rate_log + state / rate_param)
-    ) + damping_ref[...] * jnp.exp(rate_log)
-    rate_ref[...] = rate_log
-    state_ref[...] = state
-    stress_ref[...] = balance * (1.0 + excess_ref[...])
+    rate_ref[...] = rate_in[...]
 
     row_slot = pattern_ref[0:1, :]
     col_slot = pattern_ref[1:2, :]
@@ -187,10 +179,6 @@
         hit = position(block) == lax.broadcasted_iota(jnp.int32, (total, slots), 0)
         return jnp.where(hit & active, 1.0, 0.0)
 
-    row_pick[...] = onehot(row_slot, row_pick.shape[1]).T.astype(jnp.bfloat16)
-    found = onehot(col_slot, col_place.shape[0])
-    col_find[...] = found.astype(jnp.bfloat16)
-    col_place[...] = jnp.where(diagonal, 0.0, found).astype(jnp.bfloat16)
     spread[...] = jnp.where(
         lax.broadcasted_iota(jnp.int32, spread.shape, 0)
         == lax.broadcasted_iota(jnp.int32, spread.shape, 1) // EDGE,
@@ -244,6 +232,21 @@
 
         @pl.when(step == 0)
         def _():
+            normal_ref[...] = normal_in[...]
+            rate_param_ref[...] = rate_param_in[...]
+            damping_ref[...] = damping_in[...]
+            rate_log = rate_in[...]
+            state = state_in[...]
+            rate_param = rate_param_ref[...]
+            balance = normal_ref[...] * rate_param * inverse_sinh(
+                0.5 * jnp.exp(rate_log + state / rate_param)
+            ) + damping_ref[...] * jnp.exp(rate_log)
+            state_ref[...] = state
+            stress_ref[...] = balance * (1.0 + excess_ref[...])
+            row_pick[...] = onehot(row_slot, row_pick.shape[1]).T.astype(jnp.bfloat16)
+            found = onehot(col_slot, col_place.shape[0])
+            col_find[...] = found.astype(jnp.bfloat16)
+            col_place[...] = jnp.where(diagonal, 0.0, found).astype(jnp.bfloat16)
             for group in range(groups):
                 tile_copy(group).wait()
 
@@ -251,15 +254,21 @@
             tab_copy(step, "col", k, False).wait_recv()
         row_values = dot(row_pick[...], twice(row_tab[step])).astype(jnp.bfloat16)
 
-        def mirror_turn(turn, total):
-            part = pl.ds(pl.multiple_of(turn * SPAN, SPAN), SPAN)
-            product = tiles[:, part].astype(jnp.float32) * dot(row_values, spread[:, part])
-            for c in range(SPAN // LANES):
-                total = total + product[:, c * LANES : (c + 1) * LANES]
-            return total
-
-        zero = jnp.zeros((slots, LANES), jnp.float32)
-        mirror = lax.fori_loop(0, width // SPAN, mirror_turn, zero)
+        def mirror_turn(turn, carry):
+            strip = pl.ds(pl.multiple_of(turn * STRIP, STRIP), STRIP)
+            values = spread_in[strip, :]
+            total = jnp.zeros((STRIP, LANES), jnp.float32)
+            for begin in range(0, width, SPAN):
+                part = pl.ds(begin, SPAN)
+                product = tiles[strip, part].astype(jnp.float32) * dot(values, spread[:, part])
+                for c in range(SPAN // LANES):
+                    total = total + product[:, c * LANES : (c + 1) * LANES]
+            mirrored[strip, :] = total
+            return carry
+
+        spread_in[...] = row_values
+        lax.fori_loop(0, slots // STRIP, mirror_turn, 0)
+        mirror = mirrored[...]
         mirror = mirror + pltpu.roll(mirror, EDGE, 1)
         col_send[step] = paired(scatter(col_place[...], mirror), rows, half)
         for k in range(1, rows):
@@ -292,16 +301,18 @@
         wide = QUAD * EDGE
         fours = width // wide
 
-        def direct_turn(group, carry):
-            part = tiles[pl.ds(pl.multiple_of(group * GROUP, GROUP), GROUP), :]
-            stacked = jnp.concatenate(
-                [part[:, n * wide : (n + 1) * wide] for n in range(fours)], axis=0
-            )
-            product = dot(stacked, weights[group]).reshape(fours, GROUP, LANES)
-            picked[group] = jnp.sum(jnp.where(own, product, 0.0), axis=1)
+        def direct_turn(turn, carry):
+            for inner in range(QUAD):
+                group = turn * QUAD + inner
+                part = tiles[pl.ds(pl.multiple_of(group * GROUP, GROUP), GROUP), :]
+                stacked = jnp.concatenate(
+                    [part[:, n * wide : (n + 1) * wide] for n in range(fours)], axis=0
+                )
+                product = dot(stacked, weights[group]).reshape(fours, GROUP, LANES)
+                picked[group] = jnp.sum(jnp.where(own, product, 0.0), axis=1)
             return carry
 
-        lax.fori_loop(0, slots // GROUP, direct_turn, 0)
+        lax.fori_loop(0, slots // LANES, direct_turn, 0)
         narrow = lax.broadcasted_iota(jnp.int32, (fours, LANES), 1) // GROUP
         pieces = [[] for q in range(QUAD)]
         for base in range(slots // LANES):
@@ -393,6 +404,8 @@
             pltpu.VMEM((blocks_col, slots), bf16),
             pltpu.VMEM((blocks_col, slots), bf16),
             pltpu.VMEM((LANES, width), bf16),
+            pltpu.VMEM((slots, LANES), bf16),
+            pltpu.VMEM((slots, LANES), f32),
             pltpu.VMEM((slots // GROUP, QUAD * EDGE, LANES), bf16),
             pltpu.VMEM((slots // GROUP, width // (QUAD * EDGE), LANES), f32),
             pltpu.VMEM((blocks_row // LANES, LANES, LANES), f32),

time: 37.8 us -> 32.5 us (0.86)
  Pallas kernels: 36.2 us -> 31 us
    pallas_call x1, Pallas kernels: 34.6 us -> 29.3 us  [on_device(): pl.pallas_call(functools.partial(body, rows, cols), out_shape=jax.ShapeDt...]
where the time goes in v2:
time: 32.5 us; the launch traced here: 32.3 us
  Pallas kernels  31 us (95%)
  between operations  1.29 us (4%)
    pallas_call x1, Pallas kernels, on_device(): pl.pallas_call(functools.partial(body, rows, cols), out_shape=jax.ShapeDt...  29.3 us
    pallas_call x1, Pallas kernels, on_device(): pl.pallas_call(finish, out_shape=[jax.ShapeDtypeStruct(shape, f32)] * 3,...  1.65 us

profile of v2, /device:TPU:0, one launch (start us, length us, event | category | flops | bytes accessed | tf_op | source)
XLA Modules:
  0.0 32.3 jit_solution(13449617423149667930)
XLA Ops:
  1.3 29.3 %shard_map.139.final_ref = f32[6,32,128]{2,1,0:T(8,128)} custom-call(s32[1,1]{1,0:T(1,128)S(6)} %copy.15.counts_ref, s32[2,512]{1,0:T(2,128)} %bitcast.26, f32[32,128]{1,0:T(8,128)} %bitcast.17, f32[32,128]{1,0:T(8,128)} %bitcast.18, f32[32,128]{1,0:T(8,128)} %bitcast.19, f32[32,128]{1,0:T(8,128)} %bitcast.20, f32[32,128]{1,0:T(8,128)} %bitcast.21, ...), custom_call_target="tpu_custom_call" | custom-call | tf_op jit(solution)/shard_map/pallas_call | solution.py:394
  30.6 1.7 %shard_map.140 = (f32[32,128]{1,0:T(8,128)}, f32[32,128]{1,0:T(8,128)}, f32[32,128]{1,0:T(8,128)}) custom-call(f32[6,32,128]{2,1,0:T(8,128)} %shard_map.139.final_ref), custom_call_target="tpu_custom_call" | custom-call | tf_op jit(solution)/shard_map/pallas_call | solution.py:434

commit v3 on v2

--- a/solution.py
+++ b/solution.py
@@ -12,7 +12,8 @@
 EDGE = 64
 LANES = 128
 SPAN = 256
-STRIP = 128
+STRIP = 256
+BATCH = 8
 QUAD = 4
 GROUP = LANES // QUAD
 MESH = pl.DeviceIdType.MESH
@@ -24,15 +25,17 @@
     return jnp.log(value + jnp.sqrt(1.0 + value * value))
 
 
+def resistance(rate_log, state, normal_stress, rate_param, damping):
+    speed = jnp.exp(rate_log)
+    ratio = 0.5 * jnp.exp(rate_log + state / rate_param)
+    slope = -damping * speed - normal_stress * rate_param * ratio / jnp.sqrt(1.0 + ratio * ratio)
+    return damping * speed, normal_stress * rate_param * inverse_sinh(ratio), slope
+
+
 def friction_solve(rate_log, stress, state, normal_stress, rate_param, damping):
-    for turn_index in range(NEWTON):
-        speed = jnp.exp(rate_log)
-        ratio = 0.5 * jnp.exp(rate_log + state / rate_param)
-        misfit = stress - damping * speed - normal_stress * rate_param * inverse_sinh(ratio)
-        slope = -damping * speed - normal_stress * rate_param * ratio / jnp.sqrt(
-            1.0 + ratio * ratio
-        )
-        rate_log = rate_log - misfit / slope
+    for turn_index in range(NEWTON - 1):
+        viscous, friction, slope = resistance(rate_log, state, normal_stress, rate_param, damping)
+        rate_log = rate_log - (stress - viscous - friction) / slope
     return rate_log
 
 
@@ -225,10 +228,10 @@
         pushed = (speed - 1.0).astype(jnp.bfloat16)
         row_tab[step, my_col] = pushed
         col_tab[step, my_row] = pushed
+        for k in range(1, cols):
+            tab_copy(step, "col", k, True).start()
         for k in range(1, rows):
             tab_copy(step, "row", k, True).start()
-        for k in range(1, cols):
-            tab_copy(step, "col", k, True).start()
 
         @pl.when(step == 0)
         def _():
@@ -268,14 +271,12 @@
 
         spread_in[...] = row_values
         lax.fori_loop(0, slots // STRIP, mirror_turn, 0)
+        for k in range(1, rows):
+            tab_copy(step, "row", k, False).wait_recv()
         mirror = mirrored[...]
         mirror = mirror + pltpu.roll(mirror, EDGE, 1)
         col_send[step] = paired(scatter(col_place[...], mirror), rows, half)
-        for k in range(1, rows):
-            part_copy(step, "row", k).start()
-
-        for k in range(1, rows):
-            tab_copy(step, "row", k, False).wait_recv()
+
         values = lax.dot_general(
             twice(col_tab[step]),
             col_find[...],
@@ -295,6 +296,9 @@
                     axis=0,
                 ).astype(jnp.bfloat16)
 
+        for k in range(1, rows):
+            part_copy(step, "row", k).start()
+
         own = lax.broadcasted_iota(jnp.int32, (1, GROUP, LANES), 1) == (
             lax.broadcasted_iota(jnp.int32, (1, GROUP, LANES), 2) % GROUP
         )
@@ -302,8 +306,8 @@
         fours = width // wide
 
         def direct_turn(turn, carry):
-            for inner in range(QUAD):
-                group = turn * QUAD + inner
+            for inner in range(BATCH):
+                group = turn * BATCH + inner
                 part = tiles[pl.ds(pl.multiple_of(group * GROUP, GROUP), GROUP), :]
                 stacked = jnp.concatenate(
                     [part[:, n * wide : (n + 1) * wide] for n in range(fours)], axis=0
@@ -312,7 +316,7 @@
                 picked[group] = jnp.sum(jnp.where(own, product, 0.0), axis=1)
             return carry
 
-        lax.fori_loop(0, slots // LANES, direct_turn, 0)
+        lax.fori_loop(0, slots // (BATCH * GROUP), direct_turn, 0)
         narrow = lax.broadcasted_iota(jnp.int32, (fours, LANES), 1) // GROUP
         pieces = [[] for q in range(QUAD)]
         for base in range(slots // LANES):
@@ -343,29 +347,37 @@
         new_state = state + time_step * (state_param / slip_ref[...]) * (
             jnp.exp(-state / state_param) - speed
         )
+        normal_stress, rate_param, damping = normal_ref[...], rate_param_ref[...], damping_ref[...]
+        viscous, friction, slope = resistance(
+            rate_log, new_state, normal_stress, rate_param, damping
+        )
+        for k in range(1, rows):
+            tab_copy(step, "row", k, True).wait_send()
+        for k in range(1, cols):
+            tab_copy(step, "col", k, True).wait_send()
         stress_rate = col_send[step, my_row] + row_send[step, my_col]
         for k in range(1, rows):
             part_copy(step, "row", k).wait_recv()
             stress_rate = stress_rate + col_land[step, k - 1]
+        for k in range(1, rows):
+            part_copy(step, "row", k).wait_send()
         for k in range(1, cols):
             part_copy(step, "col", k).wait_recv()
             stress_rate = stress_rate + row_land[step, k - 1]
+        for k in range(1, cols):
+            part_copy(step, "col", k).wait_send()
         stress = stress_ref[...] + time_step * (stress_rate - stiff_ref[...] * (speed - 1.0))
         state_ref[...] = new_state
         stress_ref[...] = stress
+        rate_log = rate_log - (stress - viscous - friction) / slope
+        rate_ref[...] = rate_log
 
         @pl.when(step < STEPS - 1)
         def _():
             rate_ref[...] = friction_solve(
-                rate_log, stress, new_state, normal_ref[...], rate_param_ref[...], damping_ref[...]
+                rate_log, stress, new_state, normal_stress, rate_param, damping
             )
 
-        for k in range(1, rows):
-            tab_copy(step, "row", k, True).wait_send()
-            part_copy(step, "row", k).wait_send()
-        for k in range(1, cols):
-            tab_copy(step, "col", k, True).wait_send()
-            part_copy(step, "col", k).wait_send()
         return carry
 
     lax.fori_loop(0, STEPS, one_step, 0)

time: 32.5 us -> 31 us (0.954)
  Pallas kernels: 31 us -> 29.5 us
    pallas_call x1, Pallas kernels: 29.3 us -> 27.9 us  [on_device(): pl.pallas_call(functools.partial(body, rows, cols), out_shape=jax.ShapeDt...]
where the time goes in v3:
time: 31 us; the launch traced here: 30.8 us
  Pallas kernels  29.5 us (95%)
  between operations  1.29 us (4%)
    pallas_call x1, Pallas kernels, on_device(): pl.pallas_call(functools.partial(body, rows, cols), out_shape=jax.ShapeDt...  27.9 us
    pallas_call x1, Pallas kernels, on_device(): pl.pallas_call(finish, out_shape=[jax.ShapeDtypeStruct(shape, f32)] * 3,...  1.62 us

profile of v3, /device:TPU:0, one launch (start us, length us, event | category | flops | bytes accessed | tf_op | source)
XLA Modules:
  0.0 30.8 jit_solution(236431711020351061)
XLA Ops:
  1.3 27.9 %shard_map.139.final_ref = f32[6,32,128]{2,1,0:T(8,128)} custom-call(s32[1,1]{1,0:T(1,128)S(6)} %copy.15.counts_ref, s32[2,512]{1,0:T(2,128)} %bitcast.26, f32[32,128]{1,0:T(8,128)} %bitcast.17, f32[32,128]{1,0:T(8,128)} %bitcast.18, f32[32,128]{1,0:T(8,128)} %bitcast.19, f32[32,128]{1,0:T(8,128)} %bitcast.20, f32[32,128]{1,0:T(8,128)} %bitcast.21, ...), custom_call_target="tpu_custom_call" | custom-call | tf_op jit(solution)/shard_map/pallas_call | solution.py:406
  29.2 1.6 %shard_map.140 = (f32[32,128]{1,0:T(8,128)}, f32[32,128]{1,0:T(8,128)}, f32[32,128]{1,0:T(8,128)}) custom-call(f32[6,32,128]{2,1,0:T(8,128)} %shard_map.139.final_ref), custom_call_target="tpu_custom_call" | custom-call | tf_op jit(solution)/shard_map/pallas_call | solution.py:446

commit v4 on v3

--- a/solution.py
+++ b/solution.py
@@ -13,7 +13,6 @@
 LANES = 128
 SPAN = 256
 STRIP = 256
-BATCH = 8
 QUAD = 4
 GROUP = LANES // QUAD
 MESH = pl.DeviceIdType.MESH
@@ -96,10 +95,6 @@
     col_find,
     col_place,
     spread,
-    spread_in,
-    mirrored,
-    weights,
-    picked,
     turned,
     row_tab,
     col_tab,
@@ -257,26 +252,25 @@
             tab_copy(step, "col", k, False).wait_recv()
         row_values = dot(row_pick[...], twice(row_tab[step])).astype(jnp.bfloat16)
 
-        def mirror_turn(turn, carry):
-            strip = pl.ds(pl.multiple_of(turn * STRIP, STRIP), STRIP)
-            values = spread_in[strip, :]
+        mirror = []
+        for first in range(0, slots, STRIP):
+            strip = pl.ds(first, STRIP)
+            values = row_values[first : first + STRIP]
             total = jnp.zeros((STRIP, LANES), jnp.float32)
             for begin in range(0, width, SPAN):
                 part = pl.ds(begin, SPAN)
                 product = tiles[strip, part].astype(jnp.float32) * dot(values, spread[:, part])
                 for c in range(SPAN // LANES):
                     total = total + product[:, c * LANES : (c + 1) * LANES]
-            mirrored[strip, :] = total
-            return carry
-
-        spread_in[...] = row_values
-        lax.fori_loop(0, slots // STRIP, mirror_turn, 0)
+            mirror.append(total)
+        mirror = jnp.concatenate(mirror, axis=0)
         for k in range(1, rows):
             tab_copy(step, "row", k, False).wait_recv()
-        mirror = mirrored[...]
         mirror = mirror + pltpu.roll(mirror, EDGE, 1)
         col_send[step] = paired(scatter(col_place[...], mirror), rows, half)
 
+        for k in range(1, rows):
+            part_copy(step, "row", k).start()
         values = lax.dot_general(
             twice(col_tab[step]),
             col_find[...],
@@ -284,52 +278,43 @@
             preferred_element_type=jnp.float32,
         )[:EDGE]
         section = lax.broadcasted_iota(jnp.int32, (EDGE, LANES), 1) // GROUP
-        for base in range(slots // LANES):
-            part = values[:, base * LANES : (base + 1) * LANES]
+        own = lax.broadcasted_iota(jnp.int32, (1, GROUP, LANES), 1) == (
+            lax.broadcasted_iota(jnp.int32, (1, GROUP, LANES), 2) % GROUP
+        )
+        wide = QUAD * EDGE
+        fours = width // wide
+        narrow = lax.broadcasted_iota(jnp.int32, (fours, LANES), 1) // GROUP
+        sums = jnp.zeros((3 * EDGE, row_pick.shape[1]), jnp.float32)
+        for base in range(0, slots, LANES):
+            part = values[:, base : base + LANES]
             shifted = [part] + [pltpu.roll(part, n * GROUP, 1) for n in range(1, QUAD)]
+            picked = []
             for inner in range(QUAD):
-                weights[base * QUAD + inner] = jnp.concatenate(
+                weights = jnp.concatenate(
                     [
                         jnp.where(section == q, shifted[(q - inner) % QUAD], 0.0)
                         for q in range(QUAD)
                     ],
                     axis=0,
                 ).astype(jnp.bfloat16)
-
-        for k in range(1, rows):
-            part_copy(step, "row", k).start()
-
-        own = lax.broadcasted_iota(jnp.int32, (1, GROUP, LANES), 1) == (
-            lax.broadcasted_iota(jnp.int32, (1, GROUP, LANES), 2) % GROUP
-        )
-        wide = QUAD * EDGE
-        fours = width // wide
-
-        def direct_turn(turn, carry):
-            for inner in range(BATCH):
-                group = turn * BATCH + inner
-                part = tiles[pl.ds(pl.multiple_of(group * GROUP, GROUP), GROUP), :]
+                group = tiles[pl.ds(base + inner * GROUP, GROUP), :]
                 stacked = jnp.concatenate(
-                    [part[:, n * wide : (n + 1) * wide] for n in range(fours)], axis=0
+                    [group[:, n * wide : (n + 1) * wide] for n in range(fours)], axis=0
                 )
-                product = dot(stacked, weights[group]).reshape(fours, GROUP, LANES)
-                picked[group] = jnp.sum(jnp.where(own, product, 0.0), axis=1)
-            return carry
-
-        lax.fori_loop(0, slots // (BATCH * GROUP), direct_turn, 0)
-        narrow = lax.broadcasted_iota(jnp.int32, (fours, LANES), 1) // GROUP
-        pieces = [[] for q in range(QUAD)]
-        for base in range(slots // LANES):
-            parts = [picked[base * QUAD + inner] for inner in range(QUAD)]
+                product = dot(stacked, weights).reshape(fours, GROUP, LANES)
+                picked.append(jnp.sum(jnp.where(own, product, 0.0), axis=1))
+            pieces = []
             for q in range(QUAD):
                 joined = jnp.zeros((fours, LANES), jnp.float32)
                 for inner in range(QUAD):
                     shift = (inner - q) % QUAD * GROUP
-                    moved = pltpu.roll(parts[inner], shift, 1) if shift else parts[inner]
+                    moved = pltpu.roll(picked[inner], shift, 1) if shift else picked[inner]
                     joined = jnp.where(narrow == inner, moved, joined)
-                pieces[q].append(joined)
-        direct = jnp.concatenate([jnp.concatenate(part, axis=1) for part in pieces], axis=0)
-        sums = dot(jnp.concatenate(three_terms(direct), axis=0), row_pick[...])
+                pieces.append(joined)
+            direct = jnp.concatenate(pieces, axis=0)
+            sums = sums + dot(
+                jnp.concatenate(three_terms(direct), axis=0), row_pick[pl.ds(base, LANES), :]
+            )
         sums = sums[:EDGE] + sums[EDGE : 2 * EDGE] + sums[2 * EDGE :]
         for q in range(QUAD):
             for copied in range(LANES // EDGE):
@@ -416,10 +401,6 @@
             pltpu.VMEM((blocks_col, slots), bf16),
             pltpu.VMEM((blocks_col, slots), bf16),
             pltpu.VMEM((LANES, width), bf16),
-            pltpu.VMEM((slots, LANES), bf16),
-            pltpu.VMEM((slots, LANES), f32),
-            pltpu.VMEM((slots // GROUP, QUAD * EDGE, LANES), bf16),
-            pltpu.VMEM((slots // GROUP, width // (QUAD * EDGE), LANES), f32),
             pltpu.VMEM((blocks_row // LANES, LANES, LANES), f32),
             pltpu.VMEM((STEPS, cols) + shape, bf16),
             pltpu.VMEM((STEPS, rows) + shape, bf16),

time: 31 us -> 30.9 us (level)
  no operation moved by 1% of the time
where the time goes in v4:
time: 30.9 us; the launch traced here: 30.7 us
  Pallas kernels  29.4 us (95%)
  between operations  1.29 us (4%)
    pallas_call x1, Pallas kernels, on_device(): pl.pallas_call(functools.partial(body, rows, cols), out_shape=jax.ShapeDt...  27.8 us
    pallas_call x1, Pallas kernels, on_device(): pl.pallas_call(finish, out_shape=[jax.ShapeDtypeStruct(shape, f32)] * 3,...  1.62 us

profile of v4, /device:TPU:0, one launch (start us, length us, event | category | flops | bytes accessed | tf_op | source)
XLA Modules:
  0.0 30.7 jit_solution(1892411545848400339)
XLA Ops:
  1.3 27.8 %shard_map.139.final_ref = f32[6,32,128]{2,1,0:T(8,128)} custom-call(s32[1,1]{1,0:T(1,128)S(6)} %copy.15.counts_ref, s32[2,512]{1,0:T(2,128)} %bitcast.26, f32[32,128]{1,0:T(8,128)} %bitcast.17, f32[32,128]{1,0:T(8,128)} %bitcast.18, f32[32,128]{1,0:T(8,128)} %bitcast.19, f32[32,128]{1,0:T(8,128)} %bitcast.20, f32[32,128]{1,0:T(8,128)} %bitcast.21, ...), custom_call_target="tpu_custom_call" | custom-call | tf_op jit(solution)/shard_map/pallas_call | solution.py:391
  29.1 1.6 %shard_map.140 = (f32[32,128]{1,0:T(8,128)}, f32[32,128]{1,0:T(8,128)}, f32[32,128]{1,0:T(8,128)}) custom-call(f32[6,32,128]{2,1,0:T(8,128)} %shard_map.139.final_ref), custom_call_target="tpu_custom_call" | custom-call | tf_op jit(solution)/shard_map/pallas_call | solution.py:427

commit v5 on v4

--- a/solution.py
+++ b/solution.py
@@ -153,8 +153,7 @@
         copy.start()
     for group in range(groups):
         tile_copy(group).start()
-    for copy in input_copies:
-        copy.wait()
+    input_copies[0].wait()
     rate_in, state_in, excess_ref, normal_in, rate_param_in = (inputs.at[n] for n in range(5))
     state_param_ref, slip_ref, stiff_ref, damping_in = (inputs.at[n] for n in range(5, 9))
     rate_ref, state_ref, stress_ref, normal_ref, rate_param_ref, damping_ref = (
@@ -162,27 +161,6 @@
     )
     rate_ref[...] = rate_in[...]
 
-    row_slot = pattern_ref[0:1, :]
-    col_slot = pattern_ref[1:2, :]
-    active = lax.broadcasted_iota(jnp.int32, (1, slots), 1) < counts_ref[0, 0]
-    diagonal = (col_slot // per_seg == my_row) & (
-        row_slot == my_col * per_seg + col_slot % per_seg
-    )
-
-    def position(block):
-        inner = block % per_seg
-        return (block // per_seg) * per_seg + (inner % 2) * half + inner // 2
-
-    def onehot(block, total):
-        hit = position(block) == lax.broadcasted_iota(jnp.int32, (total, slots), 0)
-        return jnp.where(hit & active, 1.0, 0.0)
-
-    spread[...] = jnp.where(
-        lax.broadcasted_iota(jnp.int32, spread.shape, 0)
-        == lax.broadcasted_iota(jnp.int32, spread.shape, 1) // EDGE,
-        1.0,
-        0.0,
-    ).astype(jnp.bfloat16)
     def tab_copy(step, axis, k, sender):
         tab, sems, me, count = (
             (row_tab, sems_row_tab, my_col, cols)
@@ -230,6 +208,29 @@
 
         @pl.when(step == 0)
         def _():
+            for copy in input_copies[1:]:
+                copy.wait()
+            row_slot = pattern_ref[0:1, :]
+            col_slot = pattern_ref[1:2, :]
+            active = lax.broadcasted_iota(jnp.int32, (1, slots), 1) < counts_ref[0, 0]
+            diagonal = (col_slot // per_seg == my_row) & (
+                row_slot == my_col * per_seg + col_slot % per_seg
+            )
+
+            def position(block):
+                inner = block % per_seg
+                return (block // per_seg) * per_seg + (inner % 2) * half + inner // 2
+
+            def onehot(block, total):
+                hit = position(block) == lax.broadcasted_iota(jnp.int32, (total, slots), 0)
+                return jnp.where(hit & active, 1.0, 0.0)
+
+            spread[...] = jnp.where(
+                lax.broadcasted_iota(jnp.int32, spread.shape, 0)
+                == lax.broadcasted_iota(jnp.int32, spread.shape, 1) // EDGE,
+                1.0,
+                0.0,
+            ).astype(jnp.bfloat16)
             normal_ref[...] = normal_in[...]
             rate_param_ref[...] = rate_param_in[...]
             damping_ref[...] = damping_in[...]

time: 30.9 us -> 30.9 us (level)
  no operation moved by 1% of the time
where the time goes in v5:
time: 30.9 us; the launch traced here: 30.7 us
  Pallas kernels  29.4 us (95%)
  between operations  1.29 us (4%)
    pallas_call x1, Pallas kernels, on_device(): pl.pallas_call(functools.partial(body, rows, cols), out_shape=jax.ShapeDt...  27.8 us
    pallas_call x1, Pallas kernels, on_device(): pl.pallas_call(finish, out_shape=[jax.ShapeDtypeStruct(shape, f32)] * 3,...  1.62 us

profile of v5, /device:TPU:0, one launch (start us, length us, event | category | flops | bytes accessed | tf_op | source)
XLA Modules:
  0.0 30.7 jit_solution(16871703469598023041)
XLA Ops:
  1.3 27.8 %shard_map.139.final_ref = f32[6,32,128]{2,1,0:T(8,128)} custom-call(s32[1,1]{1,0:T(1,128)S(6)} %copy.15.counts_ref, s32[2,512]{1,0:T(2,128)} %bitcast.26, f32[32,128]{1,0:T(8,128)} %bitcast.17, f32[32,128]{1,0:T(8,128)} %bitcast.18, f32[32,128]{1,0:T(8,128)} %bitcast.19, f32[32,128]{1,0:T(8,128)} %bitcast.20, f32[32,128]{1,0:T(8,128)} %bitcast.21, ...), custom_call_target="tpu_custom_call" | custom-call | tf_op jit(solution)/shard_map/pallas_call | solution.py:392
  29.1 1.6 %shard_map.140 = (f32[32,128]{1,0:T(8,128)}, f32[32,128]{1,0:T(8,128)}, f32[32,128]{1,0:T(8,128)}) custom-call(f32[6,32,128]{2,1,0:T(8,128)} %shard_map.139.final_ref), custom_call_target="tpu_custom_call" | custom-call | tf_op jit(solution)/shard_map/pallas_call | solution.py:428
